TPU v7x, 128 devices: a whole 4x4x4 slice. The times are simulated.
128 devices in a mesh: wide: 8 (over z, core), narrow: 16 (over x, y).
Axes of the slice: x: 4, y: 4, z: 4, core: 2. Of those that a mesh axis runs over, the one named last changes fastest.
Arguments:
- tokens: bfloat16 [16384, 2048], P(('wide', 'narrow')), may hold values from -6 to 6
- out_grad: bfloat16 [16384, 2048], P(('wide', 'narrow')), may hold values from -6 to 6
- expert_ids: int32 [16384, 6], P(('wide', 'narrow')), may hold values from 0 to 63, as said below
- gates: bfloat16 [16384, 6], P(('wide', 'narrow')), may hold values from 0.049804688 to 0.5
- w_gate: bfloat16 [128, 2048, 704], P(('wide', 'narrow')), may hold values from -0.125 to 0.125
- w_up: bfloat16 [128, 2048, 704], P(('wide', 'narrow')), may hold values from -0.125 to 0.125
- w_down: bfloat16 [128, 704, 2048], P(('wide', 'narrow')), may hold values from -0.15625 to 0.15625
- gate_saved: bfloat16 [128, 1536, 704], P(('wide', 'narrow')), may hold values from -6 to 6
- up_saved: bfloat16 [128, 1536, 704], P(('wide', 'narrow')), may hold values from -6 to 6
Outputs:
- token_grad: bfloat16 [16384, 2048], P(('wide', 'narrow'))
- grad_gate: bfloat16 [128, 2048, 704], P(('wide', 'narrow'))
- grad_up: bfloat16 [128, 2048, 704], P(('wide', 'narrow'))
- grad_down: bfloat16 [128, 704, 2048], P(('wide', 'narrow'))
Inputs may be any that keep to these rules, and one draw needn't show every extreme that they name: `expert_ids`: each row names 6 different experts, 2 in each of exactly 3 of the groups of 8 consecutive experts; for every device and every group, exactly 48 of the device's tokens name experts of that group.
All inputs are finite; a program needn't handle non-finite values.
Results may differ from a plain program's by a relative error of at most 0.012.
Values may be sent and summed in bfloat16 or wider, within the bound.
No kernel may reach another device: no remote copies, remote signals or barrier semaphores. Data moves between devices by JAX's collectives and lax.ppermute only.
A program may use at most 192 MiB of HBM per device.

v0:
```python
import jax
import jax.numpy as jnp
import numpy as np
from jax import lax
from jax.experimental import pallas as pl
from jax.experimental.pallas import tpu as pltpu
from jax.sharding import PartitionSpec as P

BF = jnp.bfloat16
F32 = jnp.float32
GROUP = 16
BLOCK = 8


def dot(a, b, ca, cb, out=F32):
    return lax.dot_general(
        a, b, (((ca,), (cb,)), ((), ())), preferred_element_type=F32
    ).astype(out)


def slot_ranks(ids, experts, cap):
    choices, count = ids.shape
    expert = lax.broadcasted_iota(jnp.int32, (experts, count), 0)
    named = jnp.zeros((experts, count), F32)
    for k in range(choices):
        named = jnp.where(ids[k : k + 1] == expert, 1.0, named)
    later = (
        lax.broadcasted_iota(jnp.int32, (count, count), 0)
        < lax.broadcasted_iota(jnp.int32, (count, count), 1)
    )
    rank = dot(named.astype(BF), jnp.where(later, 1.0, 0.0).astype(BF), 1, 0)
    return jnp.where((named > 0.5) & (rank < cap), rank, -1.0)


def pick_rows(code, weight, cap):
    count = code.shape[1]
    row = lax.broadcasted_iota(jnp.int32, (2 * cap, 2 * count), 0)
    col = lax.broadcasted_iota(jnp.int32, (2 * cap, 2 * count), 1)
    slot = jnp.where(row < cap, jnp.where(col < count, row, -2), jnp.where(col < count, -2, row - cap))
    slot = slot.astype(F32)
    code = jnp.concatenate([code, code], axis=1)
    if weight is not None:
        weight = jnp.concatenate([weight, weight], axis=1)
    parts = []
    for e in range(code.shape[0]):
        worth = 1.0 if weight is None else weight[e : e + 1]
        parts += [jnp.where(code[e : e + 1] == slot, worth, 0.0)] * 2
    return jnp.concatenate(parts, axis=0).astype(BF)


def slot_kernel(experts, cap, scaled, ids, gates, values, out, stacked, rows, sems):
    count, width = values.shape
    part = width // 2
    choice = ids[...]
    code = slot_ranks(choice, experts, cap)
    weight = None
    if scaled:
        worth = gates[...].astype(F32)
        expert = lax.broadcasted_iota(jnp.int32, (experts, count), 0)
        weight = jnp.zeros((experts, count), F32)
        for k in range(choice.shape[0]):
            weight = jnp.where(choice[k : k + 1] == expert, worth[k : k + 1], weight)
    stacked[:count] = values[:, :part]
    stacked[count:] = values[:, part:]
    block = rows.shape[1]
    copies = []
    for i in range(experts // BLOCK):
        some = slice(i * BLOCK, (i + 1) * BLOCK)
        pick = pick_rows(code[some], weight[some] if scaled else None, cap)
        rows[i] = dot(pick, stacked[...], 1, 0, BF)
        copy = pltpu.make_async_copy(rows.at[i], out.at[pl.ds(i * block, block)], sems.at[i])
        copy.start()
        copies.append(copy)
    for copy in copies:
        copy.wait()


def slot_rows(ids, gates, values, experts, cap, scaled):
    count, width = values.shape
    part = width // 2
    blocks, block = experts // BLOCK, 4 * BLOCK * cap
    vmem = pl.BlockSpec(memory_space=pltpu.VMEM)
    return pl.pallas_call(
        lambda *refs: slot_kernel(experts, cap, scaled, *refs),
        in_specs=[vmem, vmem, vmem],
        out_specs=pl.BlockSpec(memory_space=pl.ANY),
        out_shape=jax.ShapeDtypeStruct((blocks * block, part), BF),
        scratch_shapes=[
            pltpu.VMEM((2 * count, part), BF),
            pltpu.VMEM((blocks, block, part), BF),
            pltpu.SemaphoreType.DMA((blocks,)),
        ],
        compiler_params=pltpu.CompilerParams(vmem_limit_bytes=56 * 2**20),
        cost_estimate=pl.CostEstimate(
            flops=2 * blocks * block * count * width,
            bytes_accessed=2 * blocks * block * part + 2 * count * width,
            transcendentals=0,
        ),
    )(ids, gates, values)


def sum_kernel(experts, cap, ids, back, out, rows, sems):
    count, width = out.shape
    part = width // 2
    blocks, block = rows.shape[:2]
    copies = [
        pltpu.make_async_copy(back.at[pl.ds(i * block, block)], rows.at[i], sems.at[i])
        for i in range(blocks)
    ]
    for copy in copies:
        copy.start()
    code = slot_ranks(ids[...], experts, cap)
    total = jnp.zeros((2 * count, part), F32)
    for i, copy in enumerate(copies):
        pick = pick_rows(code[i * BLOCK : (i + 1) * BLOCK], None, cap)
        copy.wait()
        total = total + dot(pick, rows[i], 0, 0)
    out[:, :part] = total[:count].astype(BF)
    out[:, part:] = total[count:].astype(BF)


def token_sums(ids, back, experts, cap):
    count = ids.shape[1]
    part = back.shape[1]
    blocks, block = experts // BLOCK, 4 * BLOCK * cap
    vmem = pl.BlockSpec(memory_space=pltpu.VMEM)
    return pl.pallas_call(
        lambda *refs: sum_kernel(experts, cap, *refs),
        in_specs=[vmem, pl.BlockSpec(memory_space=pl.ANY)],
        out_specs=vmem,
        out_shape=jax.ShapeDtypeStruct((count, 2 * part), BF),
        scratch_shapes=[
            pltpu.VMEM((blocks, block, part), BF),
            pltpu.SemaphoreType.DMA((blocks,)),
        ],
        compiler_params=pltpu.CompilerParams(vmem_limit_bytes=56 * 2**20),
        cost_estimate=pl.CostEstimate(
            flops=4 * blocks * block * count * part,
            bytes_accessed=2 * blocks * block * part,
            transcendentals=0,
        ),
    )(ids, back)


def half_rows(cap, half):
    row = np.arange(GROUP * cap)
    want = (row // cap * 2 + half) * cap + row % cap
    return (np.arange(GROUP * 2 * cap)[None, :] == want[:, None]).astype(jnp.bfloat16)


def local(tokens, out_grad, expert_ids, gates, w_gate, w_up, w_down, gate_saved, up_saved):
    devices = lax.axis_size("wide") * lax.axis_size("narrow")
    experts = devices // 2
    width = tokens.shape[1]
    cap = gate_saved.shape[1] // devices
    rows = devices * cap
    part = width // 2
    sides = [slice(0, part), slice(part, width)]
    picks = [jnp.asarray(half_rows(cap, half)) for half in range(2)]

    def swap(a):
        out = lax.all_to_all(
            a.reshape(devices, 2 * cap, part), ("wide", "narrow"), split_axis=0, concat_axis=0, tiled=True
        )
        return out.reshape(2 * rows, part)

    def grouped(pick, a, dim):
        a = a.reshape(devices // GROUP, -1, part)
        pick = jnp.broadcast_to(pick, (a.shape[0],) + pick.shape)
        out = lax.dot_general(
            pick, a, (((dim + 1,), (1,)), ((0,), (0,))), preferred_element_type=F32
        )
        return out.reshape(-1, part)

    def unpack(a):
        return [grouped(pick, a, 1).astype(BF) for pick in picks]

    ids, scales = expert_ids.T, gates.T
    got_dy = swap(slot_rows(ids, scales, out_grad, experts, cap, True))
    x_slots = slot_rows(ids, scales, tokens, experts, cap, False)
    x_slots, got_dy = lax.optimization_barrier((x_slots, got_dy))
    got_x = swap(x_slots)

    rows_dy = unpack(got_dy)
    gate_pre = gate_saved[0].astype(F32)
    up_pre = up_saved[0].astype(F32)
    sigma = jax.nn.sigmoid(gate_pre)
    silu = gate_pre * sigma
    act = (silu * up_pre).astype(BF)
    act_grad = sum(dot(dy, w_down[0, :, side], 1, 1) for dy, side in zip(rows_dy, sides))
    up_grad = (act_grad * silu).astype(BF)
    gate_grad = (act_grad * up_pre * sigma * (1.0 + gate_pre * (1.0 - sigma))).astype(BF)
    slot_grad = [
        (dot(gate_grad, w_gate[0, side], 1, 1) + dot(up_grad, w_up[0, side], 1, 1)).astype(BF)
        for side in sides
    ]
    packed = sum(grouped(pick, a, 0) for pick, a in zip(picks, slot_grad)).astype(BF)
    packed, got_x = lax.optimization_barrier((packed, got_x))
    back = swap(packed)
    token_grad = token_sums(ids, back, experts, cap)

    rows_x = unpack(got_x)
    grad_gate = jnp.concatenate([dot(x, gate_grad, 0, 0, BF) for x in rows_x], axis=0)
    grad_up = jnp.concatenate([dot(x, up_grad, 0, 0, BF) for x in rows_x], axis=0)
    grad_down = jnp.concatenate([dot(act, dy, 0, 0, BF) for dy in rows_dy], axis=1)
    return (token_grad, grad_gate[None], grad_up[None], grad_down[None])


def solution(mesh):
    both = ("wide", "narrow")
    flat, deep = P(both, None), P(both, None, None)
    return jax.shard_map(
        local,
        mesh=mesh,
        in_specs=(flat, flat, flat, flat, deep, deep, deep, deep, deep),
        out_specs=(flat, deep, deep, deep),
        check_vma=False,
    )
```

profile of v0, /device:TPU:1, one launch (start us, length us, event | category | flops | bytes accessed | tf_op | source)
XLA Modules:
  0.0 261.6 jit_solution(8802566844313792307)
XLA Ops:
  0.6 4.2 %shard_map.139 = bf16[3072,1024]{1,0:T(8,128)(2,1)} custom-call(s32[6,128]{1,0:T(8,128)} %bitcast.133, bf16[6,128]{1,0:T(8,128)(2,1)} %bitcast.136, bf16[128,2048]{1,0:T(8,128)(2,1)} %refs_2_.3), custom_call_target="tpu_custom_call" | custom-call | flops 1610612736 | bytes 6815744 | tf_op jit(solution)/shard_map/pallas_call | solution.py:83
  4.9 11.9 %all-to-all-start = ((bf16[128,24,1024]{2,1,0:T(8,128)(2,1)}), bf16[128,24,1024]{2,1,0:T(8,128)(2,1)}, u32[]{:S(2)}, u32[]{:S(2)}) async-start(bf16[128,24,1024]{2,1,0:T(8,128)(2,1)} %bitcast.121), calls=%async_computation | async-start | bytes 12582912 | tf_op jit(solution)/shard_map/all_to_all | solution.py:162
  16.8 4.2 %shard_map.138 = bf16[3072,1024]{1,0:T(8,128)(2,1)} custom-call(s32[6,128]{1,0:T(8,128)} %bitcast.134, bf16[6,128]{1,0:T(8,128)(2,1)} %bitcast.137, bf16[128,2048]{1,0:T(8,128)(2,1)} %refs_2_.2), custom_call_target="tpu_custom_call" | custom-call | flops 1610612736 | bytes 6815744 | tf_op jit(solution)/shard_map/pallas_call | solution.py:83
  21.0 71.3 %all-to-all-done = bf16[128,24,1024]{2,1,0:T(8,128)(2,1)} async-done(((bf16[128,24,1024]{2,1,0:T(8,128)(2,1)}), bf16[128,24,1024]{2,1,0:T(8,128)(2,1)}, u32[]{:S(2)}, u32[]{:S(2)}) %all-to-all-start) | async-done | bytes 6291488 | tf_op jit(solution)/shard_map/all_to_all | solution.py:162
  92.3 6.5 %all-to-all-start.1 = ((bf16[128,24,1024]{2,1,0:T(8,128)(2,1)}), bf16[128,24,1024]{2,1,0:T(8,128)(2,1)}, u32[]{:S(2)}, u32[]{:S(2)}) async-start(bf16[128,24,1024]{2,1,0:T(8,128)(2,1)} %bitcast.120), calls=%async_computation.1 | async-start | bytes 12582912 | tf_op jit(solution)/shard_map/all_to_all | solution.py:162
  98.8 0.0 copy-start.2
  98.8 4.6 %convolution_convert_fusion.3 = bf16[8,1024,192]{1,2,0:T(8,128)(2,1)S(1)} fusion(bf16[8,384,1024]{2,1,0:T(8,128)(2,1)} %bitcast.4, bf16[192,384]{1,0:T(8,128)(2,1)S(1)} %copy-done.1), kind=kOutput, calls=%fused_computation.32 | convolution fusion | flops 1209532416 | bytes 9584640 | tf_op jit(solution)/shard_map/dot_general | solution.py:170
  103.5 5.8 %convolution_convert_fusion.2 = bf16[8,1024,192]{1,2,0:T(8,128)(2,1)S(1)} fusion(bf16[8,384,1024]{2,1,0:T(8,128)(2,1)} %bitcast.4, bf16[192,384]{1,0:T(8,128)(2,1)S(1)} %copy-done.2), kind=kOutput, calls=%fused_computation.31 | convolution fusion | flops 1209532416 | bytes 9584640 | tf_op jit(solution)/shard_map/dot_general | solution.py:170
  109.3 0.0 copy-start.6
  109.3 2.4 fusion.34
  111.8 4.5 %fusion.13 = (bf16[1536,704]{0,1:T(8,128)(2,1)S(1)}, bf16[1536,704]{0,1:T(8,128)(2,1)S(1)}) fusion(bf16[1,1536,704]{1,2,0:T(8,128)(2,1)S(1)} %copy-done.6, bf16[1,1536,704]{1,2,0:T(8,128)(2,1)S(1)} %copy-done.8, f32[1536,704]{0,1:T(8,128)S(1)} %fusion.34, bf16[1536,1024]{1,0:T(8,128)(2,1)S(1)} %bitcast.123, bf16[1,704,2048]{2,1,0:T(8,128)(2,1)S(1)} %copy-done.3), kind=kOutput, calls=%fused_computation.21 | convolution fusion | flops 2231894016 | bytes 17563648 | tf_op jit(solution)/shard_map/dot_general | solution.py:16
  116.3 0.0 copy-start.10
  116.3 2.7 %fusion.28 = f32[1536,1024]{1,0:T(8,128)S(1)} fusion(bf16[1536,704]{0,1:T(8,128)(2,1)S(1)} %get-tuple-element.13, bf16[1,2048,704]{1,2,0:T(8,128)(2,1)S(1)} %copy-done.4), kind=kOutput, calls=%fused_computation.44 | convolution fusion | flops 2214592512 | bytes 9895936 | tf_op jit(solution)/shard_map/dot_general | solution.py:16
  119.0 2.7 %fusion.31 = f32[1536,1024]{1,0:T(8,128)S(1)} fusion(bf16[1536,704]{0,1:T(8,128)(2,1)S(1)} %get-tuple-element.13, bf16[1,2048,704]{1,2,0:T(8,128)(2,1)S(1)} %copy-done.4), kind=kOutput, calls=%fused_computation.47 | convolution fusion | flops 2214592512 | bytes 9895936 | tf_op jit(solution)/shard_map/dot_general | solution.py:16
  121.7 3.2 %add_convert_fusion.2 = bf16[1536,1024]{1,0:T(8,128)(2,1)S(1)} fusion(f32[1536,1024]{1,0:T(8,128)S(1)} %fusion.31, bf16[1536,704]{0,1:T(8,128)(2,1)S(1)} %get-tuple-element.12, bf16[1,2048,704]{1,2,0:T(8,128)(2,1)S(1)} %copy-done.5), kind=kOutput, calls=%fused_computation.8 | convolution fusion | flops 2217738240 | bytes 13041664 | tf_op jit(solution)/shard_map/dot_general | solution.py:16
  125.0 6.4 %fusion.46 = f32[8,1024,384]{1,2,0:T(8,128)} fusion(bf16[8,192,1024]{2,1,0:T(8,128)(2,1)S(1)} %bitcast.132, bf16[192,384]{1,0:T(8,128)(2,1)S(1)} %copy-done.1), kind=kOutput, calls=%fused_computation.62 | convolution fusion | flops 1207959552 | bytes 15876096 | tf_op jit(solution)/shard_map/dot_general | solution.py:170
  131.4 3.0 %add_convert_fusion.1 = bf16[1536,1024]{1,0:T(8,128)(2,1)S(1)} fusion(f32[1536,1024]{1,0:T(8,128)S(1)} %fusion.28, bf16[1536,704]{0,1:T(8,128)(2,1)S(1)} %get-tuple-element.12, bf16[1,2048,704]{1,2,0:T(8,128)(2,1)S(1)} %copy-done.5), kind=kOutput, calls=%fused_computation.7 | convolution fusion | flops 2217738240 | bytes 13041664 | tf_op jit(solution)/shard_map/dot_general | solution.py:16
  134.4 9.3 %add_convert_fusion = bf16[8,1024,384]{1,2,0:T(8,128)(2,1)} fusion(f32[8,1024,384]{1,2,0:T(8,128)} %fusion.46, bf16[8,192,1024]{2,1,0:T(8,128)(2,1)S(1)} %bitcast.131, bf16[192,384]{1,0:T(8,128)(2,1)S(1)} %copy-done.2), kind=kOutput, calls=%fused_computation | convolution fusion | flops 1214251008 | bytes 22167552 | tf_op jit(solution)/shard_map/dot_general | solution.py:170
  143.8 30.5 %all-to-all-done.1 = bf16[128,24,1024]{2,1,0:T(8,128)(2,1)} async-done(((bf16[128,24,1024]{2,1,0:T(8,128)(2,1)}), bf16[128,24,1024]{2,1,0:T(8,128)(2,1)}, u32[]{:S(2)}, u32[]{:S(2)}) %all-to-all-start.1) | async-done | bytes 6291488 | tf_op jit(solution)/shard_map/all_to_all | solution.py:162
  174.3 5.9 %all-to-all-start.2 = ((bf16[128,24,1024]{2,1,0:T(8,128)(2,1)}), bf16[128,24,1024]{2,1,0:T(8,128)(2,1)}, u32[]{:S(2)}, u32[]{:S(2)}) async-start(bf16[128,24,1024]{2,1,0:T(8,128)(2,1)} %bitcast.122), calls=%async_computation.2 | async-start | bytes 12582912 | tf_op jit(solution)/shard_map/all_to_all | solution.py:162
  180.2 6.0 %fusion.21 = bf16[704,1024]{1,0:T(8,128)(2,1)S(1)} fusion(bf16[1536,1024]{1,0:T(8,128)(2,1)} %bitcast.126, bf16[1,1536,704]{1,2,0:T(8,128)(2,1)} %param.19, bf16[1,1536,704]{1,2,0:T(8,128)(2,1)} %param.18), kind=kOutput, calls=%fused_computation.37 | convolution fusion | flops 2223964160 | bytes 8912896 | tf_op jit(solution)/shard_map/dot_general | solution.py:16
  186.3 2.8 %fusion.24 = bf16[704,1024]{1,0:T(8,128)(2,1)S(1)} fusion(bf16[1536,1024]{1,0:T(8,128)(2,1)S(1)} %bitcast.124, bf16[1,1536,704]{1,2,0:T(8,128)(2,1)S(1)} %copy-done.9, bf16[1,1536,704]{1,2,0:T(8,128)(2,1)S(1)} %copy-done.7), kind=kOutput, calls=%fused_computation.38 | convolution fusion | flops 2223964160 | bytes 8912896 | tf_op jit(solution)/shard_map/dot_general | solution.py:16
  189.1 1.8 maximum_bitcast_fusion.2
  190.9 4.6 %convolution_convert_fusion.1 = bf16[8,1024,192]{1,2,0:T(8,128)(2,1)S(1)} fusion(bf16[8,384,1024]{2,1,0:T(8,128)(2,1)} %bitcast.25, bf16[192,384]{1,0:T(8,128)(2,1)S(1)} %copy-done.1), kind=kOutput, calls=%fused_computation.30 | convolution fusion | flops 1209532416 | bytes 9584640 | tf_op jit(solution)/shard_map/dot_general | solution.py:170
  195.5 4.7 %convolution_convert_fusion = bf16[8,1024,192]{1,2,0:T(8,128)(2,1)S(1)} fusion(bf16[8,384,1024]{2,1,0:T(8,128)(2,1)} %bitcast.25, bf16[192,384]{1,0:T(8,128)(2,1)S(1)} %copy-done.2), kind=kOutput, calls=%fused_computation.29 | convolution fusion | flops 1209532416 | bytes 9584640 | tf_op jit(solution)/shard_map/dot_general | solution.py:170
  200.3 2.4 convolution_convert_fusion.7
  202.7 2.4 convolution_convert_fusion.5
  205.1 2.7 %convolution_convert_fusion.4 = bf16[1024,704]{0,1:T(8,128)(2,1)S(1)} fusion(bf16[1536,704]{0,1:T(8,128)(2,1)S(1)} %copy-done.13, bf16[1536,1024]{1,0:T(8,128)(2,1)S(1)} %bitcast.127), kind=kOutput, calls=%fused_computation.39 | convolution fusion | flops 2215313408 | bytes 6750208 | tf_op jit(solution)/shard_map/dot_general | solution.py:16
  207.9 2.4 convolution_convert_fusion.6
  210.3 2.8 %maximum_bitcast_fusion = (bf16[1,2048,704]{1,2,0:T(8,128)(2,1)}, bf16[1,2048,704]{1,2,0:T(8,128)(2,1)}) fusion(bf16[1024,704]{0,1:T(8,128)(2,1)S(1)} %convolution_convert_fusion.6, bf16[1024,704]{0,1:T(8,128)(2,1)S(1)} %convolution_convert_fusion.7, bf16[1024,704]{0,1:T(8,128)(2,1)S(1)} %convolution_convert_fusion.4, ...), kind=kLoop, calls=%fused_computation.26 | loop fusion | flops 11534336 | bytes 11534336 | tf_op jit(solution)/shard_map/broadcast_in_dim | solution.py:206
  213.1 42.4 %all-to-all-done.2 = bf16[128,24,1024]{2,1,0:T(8,128)(2,1)} async-done(((bf16[128,24,1024]{2,1,0:T(8,128)(2,1)}), bf16[128,24,1024]{2,1,0:T(8,128)(2,1)}, u32[]{:S(2)}, u32[]{:S(2)}) %all-to-all-start.2) | async-done | bytes 6291488 | tf_op jit(solution)/shard_map/all_to_all | solution.py:162
  255.5 5.8 %shard_map.140 = bf16[128,2048]{1,0:T(8,128)(2,1)} custom-call(s32[6,128]{1,0:T(8,128)} %bitcast.135, bf16[3072,1024]{1,0:T(8,128)(2,1)} %bitcast.24.refs_1_), custom_call_target="tpu_custom_call" | custom-call | flops 1610612736 | bytes 6291456 | tf_op jit(solution)/shard_map/pallas_call | solution.py:127
  (25 shorter events, 0.1 us)
Async XLA Ops:
  4.9 87.5 %all-to-all-start = ((bf16[128,24,1024]{2,1,0:T(8,128)(2,1)}), bf16[128,24,1024]{2,1,0:T(8,128)(2,1)}, u32[]{:S(2)}, u32[]{:S(2)}) async-start(bf16[128,24,1024]{2,1,0:T(8,128)(2,1)} %bitcast.121), calls=%async_computation | async-start | bytes 12582912 | tf_op jit(solution)/shard_map/all_to_all | solution.py:162
  92.3 6.5 %copy-start.1 = (bf16[192,384]{1,0:T(8,128)(2,1)S(1)}, bf16[192,384]{1,0:T(8,128)(2,1)}, u32[]{:S(2)}) copy-start(bf16[192,384]{1,0:T(8,128)(2,1)} %constant.6.clone) | copy-start | bytes 442372
  92.3 81.9 %all-to-all-start.1 = ((bf16[128,24,1024]{2,1,0:T(8,128)(2,1)}), bf16[128,24,1024]{2,1,0:T(8,128)(2,1)}, u32[]{:S(2)}, u32[]{:S(2)}) async-start(bf16[128,24,1024]{2,1,0:T(8,128)(2,1)} %bitcast.120), calls=%async_computation.1 | async-start | bytes 12582912 | tf_op jit(solution)/shard_map/all_to_all | solution.py:162
  98.8 4.6 %copy-start.2 = (bf16[192,384]{1,0:T(8,128)(2,1)S(1)}, bf16[192,384]{1,0:T(8,128)(2,1)}, u32[]{:S(2)}) copy-start(bf16[192,384]{1,0:T(8,128)(2,1)} %constant.7.clone) | copy-start | bytes 442372
  103.5 5.8 %copy-start = (bf16[8,1024,192]{1,2,0:T(8,128)(2,1)}, bf16[8,1024,192]{1,2,0:T(8,128)(2,1)S(1)}, u32[]{:S(2)}) copy-start(bf16[8,1024,192]{1,2,0:T(8,128)(2,1)S(1)} %convolution_convert_fusion.3) | copy-start | bytes 9437188
  103.5 5.8 %copy-start.3 = (bf16[1,704,2048]{2,1,0:T(8,128)(2,1)S(1)}, bf16[1,704,2048]{2,1,0:T(8,128)(2,1)}, u32[]{:S(2)}) copy-start(bf16[1,704,2048]{2,1,0:T(8,128)(2,1)} %param.17) | copy-start | bytes 8650756
  109.3 2.5 copy-start.6
  109.3 2.5 copy-start.8
  111.8 4.5 %copy-start.4 = (bf16[1,2048,704]{1,2,0:T(8,128)(2,1)S(1)}, bf16[1,2048,704]{1,2,0:T(8,128)(2,1)}, u32[]{:S(2)}) copy-start(bf16[1,2048,704]{1,2,0:T(8,128)(2,1)} %param.15) | copy-start | bytes 8650756
  116.3 2.7 %copy-start.10 = (bf16[1536,704]{0,1:T(8,128)(2,1)}, bf16[1536,704]{0,1:T(8,128)(2,1)S(1)}, u32[]{:S(2)}) copy-start(bf16[1536,704]{0,1:T(8,128)(2,1)S(1)} %get-tuple-element.13) | copy-start | bytes 6488068
  116.3 15.1 %copy-start.12 = (bf16[1536,704]{0,1:T(8,128)(2,1)}, bf16[1536,704]{0,1:T(8,128)(2,1)S(1)}, u32[]{:S(2)}) copy-start(bf16[1536,704]{0,1:T(8,128)(2,1)S(1)} %get-tuple-element.12) | copy-start | bytes 6488068
  119.0 2.7 %copy-start.5 = (bf16[1,2048,704]{1,2,0:T(8,128)(2,1)S(1)}, bf16[1,2048,704]{1,2,0:T(8,128)(2,1)}, u32[]{:S(2)}) copy-start(bf16[1,2048,704]{1,2,0:T(8,128)(2,1)} %param.16) | copy-start | bytes 8650756
  174.3 81.3 %all-to-all-start.2 = ((bf16[128,24,1024]{2,1,0:T(8,128)(2,1)}), bf16[128,24,1024]{2,1,0:T(8,128)(2,1)}, u32[]{:S(2)}, u32[]{:S(2)}) async-start(bf16[128,24,1024]{2,1,0:T(8,128)(2,1)} %bitcast.122), calls=%async_computation.2 | async-start | bytes 12582912 | tf_op jit(solution)/shard_map/all_to_all | solution.py:162
  180.2 6.1 %copy-start.7 = (bf16[1,1536,704]{1,2,0:T(8,128)(2,1)S(1)}, bf16[1,1536,704]{1,2,0:T(8,128)(2,1)}, u32[]{:S(2)}) copy-start(bf16[1,1536,704]{1,2,0:T(8,128)(2,1)} %param.18) | copy-start | bytes 6488068
  180.2 6.1 %copy-start.9 = (bf16[1,1536,704]{1,2,0:T(8,128)(2,1)S(1)}, bf16[1,1536,704]{1,2,0:T(8,128)(2,1)}, u32[]{:S(2)}) copy-start(bf16[1,1536,704]{1,2,0:T(8,128)(2,1)} %param.19) | copy-start | bytes 6488068
  195.5 4.8 %copy-start.11 = (bf16[1536,704]{0,1:T(8,128)(2,1)S(1)}, bf16[1536,704]{0,1:T(8,128)(2,1)}, u32[]{:S(2)}) copy-start(bf16[1536,704]{0,1:T(8,128)(2,1)} %copy-done.10) | copy-start | bytes 6488068
  200.3 2.4 copy-start.13
where the time goes:
time: 266 us; the launch traced here: 262 us
  waiting for transfers between devices  144 us (54%)
  matrix products  72.7 us (27%)
  starting transfers between devices  24.3 us (9%)
  Pallas kernels  14.3 us (5%)
  other arithmetic  4.68 us (2%)
    all_to_all x3, waiting for transfers between devices, swap(): lax.all_to_all(a.reshape(devices, 2 * cap, part), ('wide', 'narrow'), spl...  144 us
    dot_general x12, matrix products, dot(): lax.dot_general(a, b, (((ca,), (cb,)), ((), ())), preferred_element_type=...  37.3 us
    dot_general x6, matrix products, grouped(): lax.dot_general(pick, a, (((dim + 1,), (1,)), ((0,), (0,))), preferred_el...  35.4 us
    all_to_all x3, starting transfers between devices, swap(): lax.all_to_all(a.reshape(devices, 2 * cap, part), ('wide', 'narrow'), spl...  24.3 us
    pallas_call x2, Pallas kernels, slot_rows(): pl.pallas_call(lambda *refs: slot_kernel(experts, cap, scaled, *refs), in...  8.47 us
    pallas_call x1, Pallas kernels, token_sums(): pl.pallas_call(lambda *refs: sum_kernel(experts, cap, *refs), in_specs=[v...  5.81 us
  transfers between devices with their start and end apart: 3, of which 3 were waited for; matrix products, arithmetic and copies ran while one was open for 30% of the time, Pallas kernels for 2%

commit v1 on v0

--- a/solution.py
+++ b/solution.py
@@ -48,9 +48,17 @@
     return jnp.concatenate(parts, axis=0).astype(BF)
 
 
-def slot_kernel(experts, cap, scaled, ids, gates, values, out, stacked, rows, sems):
+def slot_kernel(experts, cap, scaled, ids, gates, values, out, stacked, rows, sems, load_sems):
     count, width = values.shape
     part = width // 2
+    loads = [
+        pltpu.make_async_copy(
+            values.at[:, pl.ds(half * part, part)], stacked.at[pl.ds(half * count, count)], load_sems.at[half]
+        )
+        for half in range(2)
+    ]
+    for load in loads:
+        load.start()
     choice = ids[...]
     code = slot_ranks(choice, experts, cap)
     weight = None
@@ -60,8 +68,8 @@
         weight = jnp.zeros((experts, count), F32)
         for k in range(choice.shape[0]):
             weight = jnp.where(choice[k : k + 1] == expert, worth[k : k + 1], weight)
-    stacked[:count] = values[:, :part]
-    stacked[count:] = values[:, part:]
+    for load in loads:
+        load.wait()
     block = rows.shape[1]
     copies = []
     for i in range(experts // BLOCK):
@@ -82,13 +90,14 @@
     vmem = pl.BlockSpec(memory_space=pltpu.VMEM)
     return pl.pallas_call(
         lambda *refs: slot_kernel(experts, cap, scaled, *refs),
-        in_specs=[vmem, vmem, vmem],
+        in_specs=[vmem, vmem, pl.BlockSpec(memory_space=pl.ANY)],
         out_specs=pl.BlockSpec(memory_space=pl.ANY),
         out_shape=jax.ShapeDtypeStruct((blocks * block, part), BF),
         scratch_shapes=[
             pltpu.VMEM((2 * count, part), BF),
             pltpu.VMEM((blocks, block, part), BF),
             pltpu.SemaphoreType.DMA((blocks,)),
+            pltpu.SemaphoreType.DMA((2,)),
         ],
         compiler_params=pltpu.CompilerParams(vmem_limit_bytes=56 * 2**20),
         cost_estimate=pl.CostEstimate(
@@ -102,19 +111,21 @@
 def sum_kernel(experts, cap, ids, back, out, rows, sems):
     count, width = out.shape
     part = width // 2
-    blocks, block = rows.shape[:2]
-    copies = [
-        pltpu.make_async_copy(back.at[pl.ds(i * block, block)], rows.at[i], sems.at[i])
-        for i in range(blocks)
-    ]
+    blocks = experts // BLOCK
+    block = rows.shape[0] // blocks
+    copies = []
+    for i in range(blocks):
+        place = pl.ds(i * block, block)
+        copies.append(pltpu.make_async_copy(back.at[place], rows.at[place], sems.at[i]))
     for copy in copies:
         copy.start()
     code = slot_ranks(ids[...], experts, cap)
     total = jnp.zeros((2 * count, part), F32)
-    for i, copy in enumerate(copies):
-        pick = pick_rows(code[i * BLOCK : (i + 1) * BLOCK], None, cap)
-        copy.wait()
-        total = total + dot(pick, rows[i], 0, 0)
+    for i in range(0, blocks, 2):
+        pick = pick_rows(code[i * BLOCK : (i + 2) * BLOCK], None, cap)
+        copies[i].wait()
+        copies[i + 1].wait()
+        total = total + dot(pick, rows[i * block : (i + 2) * block], 0, 0)
     out[:, :part] = total[:count].astype(BF)
     out[:, part:] = total[count:].astype(BF)
 
@@ -130,7 +141,7 @@
         out_specs=vmem,
         out_shape=jax.ShapeDtypeStruct((count, 2 * part), BF),
         scratch_shapes=[
-            pltpu.VMEM((blocks, block, part), BF),
+            pltpu.VMEM((blocks * block, part), BF),
             pltpu.SemaphoreType.DMA((blocks,)),
         ],
         compiler_params=pltpu.CompilerParams(vmem_limit_bytes=56 * 2**20),

time: 266 us -> 266 us (level)
  no operation moved by 1% of the time
where the time goes in v1:
time: 266 us; the launch traced here: 262 us
  waiting for transfers between devices  144 us (54%)
  matrix products  72.7 us (27%)
  starting transfers between devices  24.3 us (9%)
  Pallas kernels  15.1 us (6%)
  other arithmetic  4.68 us (2%)
    all_to_all x3, waiting for transfers between devices, swap(): lax.all_to_all(a.reshape(devices, 2 * cap, part), ('wide', 'narrow'), spl...  144 us
    dot_general x12, matrix products, dot(): lax.dot_general(a, b, (((ca,), (cb,)), ((), ())), preferred_element_type=...  37.3 us
    dot_general x6, matrix products, grouped(): lax.dot_general(pick, a, (((dim + 1,), (1,)), ((0,), (0,))), preferred_el...  35.4 us
    all_to_all x3, starting transfers between devices, swap(): lax.all_to_all(a.reshape(devices, 2 * cap, part), ('wide', 'narrow'), spl...  24.3 us
    pallas_call x2, Pallas kernels, slot_rows(): pl.pallas_call(lambda *refs: slot_kernel(experts, cap, scaled, *refs), in...  9.61 us
    pallas_call x1, Pallas kernels, token_sums(): pl.pallas_call(lambda *refs: sum_kernel(experts, cap, *refs), in_specs=[v...  5.51 us
  transfers between devices with their start and end apart: 3, of which 3 were waited for; matrix products, arithmetic and copies ran while one was open for 30% of the time, Pallas kernels for 2%

profile of v1, /device:TPU:1, one launch (start us, length us, event | category | flops | bytes accessed | tf_op | source)
XLA Modules:
  0.0 261.9 jit_solution(15993774397407407170)
XLA Ops:
  0.6 4.8 %shard_map.139 = bf16[3072,1024]{1,0:T(8,128)(2,1)} custom-call(s32[6,128]{1,0:T(8,128)} %bitcast.133, bf16[6,128]{1,0:T(8,128)(2,1)} %bitcast.136, bf16[128,2048]{1,0:T(8,128)(2,1)} %refs_2_.3), custom_call_target="tpu_custom_call" | custom-call | flops 1610612736 | bytes 6815744 | tf_op jit(solution)/shard_map/pallas_call | solution.py:91
  5.4 11.9 %all-to-all-start = ((bf16[128,24,1024]{2,1,0:T(8,128)(2,1)}), bf16[128,24,1024]{2,1,0:T(8,128)(2,1)}, u32[]{:S(2)}, u32[]{:S(2)}) async-start(bf16[128,24,1024]{2,1,0:T(8,128)(2,1)} %bitcast.121), calls=%async_computation | async-start | bytes 12582912 | tf_op jit(solution)/shard_map/all_to_all | solution.py:173
  17.3 4.8 %shard_map.138 = bf16[3072,1024]{1,0:T(8,128)(2,1)} custom-call(s32[6,128]{1,0:T(8,128)} %bitcast.134, bf16[6,128]{1,0:T(8,128)(2,1)} %bitcast.137, bf16[128,2048]{1,0:T(8,128)(2,1)} %refs_2_.2), custom_call_target="tpu_custom_call" | custom-call | flops 1610612736 | bytes 6815744 | tf_op jit(solution)/shard_map/pallas_call | solution.py:91
  22.2 70.7 %all-to-all-done = bf16[128,24,1024]{2,1,0:T(8,128)(2,1)} async-done(((bf16[128,24,1024]{2,1,0:T(8,128)(2,1)}), bf16[128,24,1024]{2,1,0:T(8,128)(2,1)}, u32[]{:S(2)}, u32[]{:S(2)}) %all-to-all-start) | async-done | bytes 6291488 | tf_op jit(solution)/shard_map/all_to_all | solution.py:173
  92.9 6.5 %all-to-all-start.1 = ((bf16[128,24,1024]{2,1,0:T(8,128)(2,1)}), bf16[128,24,1024]{2,1,0:T(8,128)(2,1)}, u32[]{:S(2)}, u32[]{:S(2)}) async-start(bf16[128,24,1024]{2,1,0:T(8,128)(2,1)} %bitcast.120), calls=%async_computation.1 | async-start | bytes 12582912 | tf_op jit(solution)/shard_map/all_to_all | solution.py:173
  99.4 0.0 copy-start.2
  99.4 4.6 %convolution_convert_fusion.3 = bf16[8,1024,192]{1,2,0:T(8,128)(2,1)S(1)} fusion(bf16[8,384,1024]{2,1,0:T(8,128)(2,1)} %bitcast.4, bf16[192,384]{1,0:T(8,128)(2,1)S(1)} %copy-done.1), kind=kOutput, calls=%fused_computation.32 | convolution fusion | flops 1209532416 | bytes 9584640 | tf_op jit(solution)/shard_map/dot_general | solution.py:181
  104.1 0.0 copy-start.3
  104.1 5.8 %convolution_convert_fusion.2 = bf16[8,1024,192]{1,2,0:T(8,128)(2,1)S(1)} fusion(bf16[8,384,1024]{2,1,0:T(8,128)(2,1)} %bitcast.4, bf16[192,384]{1,0:T(8,128)(2,1)S(1)} %copy-done.2), kind=kOutput, calls=%fused_computation.31 | convolution fusion | flops 1209532416 | bytes 9584640 | tf_op jit(solution)/shard_map/dot_general | solution.py:181
  109.9 0.0 copy-start.6
  109.9 2.4 fusion.34
  112.4 4.5 %fusion.13 = (bf16[1536,704]{0,1:T(8,128)(2,1)S(1)}, bf16[1536,704]{0,1:T(8,128)(2,1)S(1)}) fusion(bf16[1,1536,704]{1,2,0:T(8,128)(2,1)S(1)} %copy-done.6, bf16[1,1536,704]{1,2,0:T(8,128)(2,1)S(1)} %copy-done.8, f32[1536,704]{0,1:T(8,128)S(1)} %fusion.34, bf16[1536,1024]{1,0:T(8,128)(2,1)S(1)} %bitcast.123, bf16[1,704,2048]{2,1,0:T(8,128)(2,1)S(1)} %copy-done.3), kind=kOutput, calls=%fused_computation.21 | convolution fusion | flops 2231894016 | bytes 17563648 | tf_op jit(solution)/shard_map/dot_general | solution.py:16
  116.9 2.7 %fusion.28 = f32[1536,1024]{1,0:T(8,128)S(1)} fusion(bf16[1536,704]{0,1:T(8,128)(2,1)S(1)} %get-tuple-element.13, bf16[1,2048,704]{1,2,0:T(8,128)(2,1)S(1)} %copy-done.4), kind=kOutput, calls=%fused_computation.44 | convolution fusion | flops 2214592512 | bytes 9895936 | tf_op jit(solution)/shard_map/dot_general | solution.py:16
  119.6 2.7 %fusion.31 = f32[1536,1024]{1,0:T(8,128)S(1)} fusion(bf16[1536,704]{0,1:T(8,128)(2,1)S(1)} %get-tuple-element.13, bf16[1,2048,704]{1,2,0:T(8,128)(2,1)S(1)} %copy-done.4), kind=kOutput, calls=%fused_computation.47 | convolution fusion | flops 2214592512 | bytes 9895936 | tf_op jit(solution)/shard_map/dot_general | solution.py:16
  122.3 3.2 %add_convert_fusion.2 = bf16[1536,1024]{1,0:T(8,128)(2,1)S(1)} fusion(f32[1536,1024]{1,0:T(8,128)S(1)} %fusion.31, bf16[1536,704]{0,1:T(8,128)(2,1)S(1)} %get-tuple-element.12, bf16[1,2048,704]{1,2,0:T(8,128)(2,1)S(1)} %copy-done.5), kind=kOutput, calls=%fused_computation.8 | convolution fusion | flops 2217738240 | bytes 13041664 | tf_op jit(solution)/shard_map/dot_general | solution.py:16
  125.5 6.4 %fusion.46 = f32[8,1024,384]{1,2,0:T(8,128)} fusion(bf16[8,192,1024]{2,1,0:T(8,128)(2,1)S(1)} %bitcast.132, bf16[192,384]{1,0:T(8,128)(2,1)S(1)} %copy-done.1), kind=kOutput, calls=%fused_computation.62 | convolution fusion | flops 1207959552 | bytes 15876096 | tf_op jit(solution)/shard_map/dot_general | solution.py:181
  131.9 3.0 %add_convert_fusion.1 = bf16[1536,1024]{1,0:T(8,128)(2,1)S(1)} fusion(f32[1536,1024]{1,0:T(8,128)S(1)} %fusion.28, bf16[1536,704]{0,1:T(8,128)(2,1)S(1)} %get-tuple-element.12, bf16[1,2048,704]{1,2,0:T(8,128)(2,1)S(1)} %copy-done.5), kind=kOutput, calls=%fused_computation.7 | convolution fusion | flops 2217738240 | bytes 13041664 | tf_op jit(solution)/shard_map/dot_general | solution.py:16
  135.0 9.3 %add_convert_fusion = bf16[8,1024,384]{1,2,0:T(8,128)(2,1)} fusion(f32[8,1024,384]{1,2,0:T(8,128)} %fusion.46, bf16[8,192,1024]{2,1,0:T(8,128)(2,1)S(1)} %bitcast.131, bf16[192,384]{1,0:T(8,128)(2,1)S(1)} %copy-done.2), kind=kOutput, calls=%fused_computation | convolution fusion | flops 1214251008 | bytes 22167552 | tf_op jit(solution)/shard_map/dot_general | solution.py:181
  144.3 30.5 %all-to-all-done.1 = bf16[128,24,1024]{2,1,0:T(8,128)(2,1)} async-done(((bf16[128,24,1024]{2,1,0:T(8,128)(2,1)}), bf16[128,24,1024]{2,1,0:T(8,128)(2,1)}, u32[]{:S(2)}, u32[]{:S(2)}) %all-to-all-start.1) | async-done | bytes 6291488 | tf_op jit(solution)/shard_map/all_to_all | solution.py:173
  174.8 5.9 %all-to-all-start.2 = ((bf16[128,24,1024]{2,1,0:T(8,128)(2,1)}), bf16[128,24,1024]{2,1,0:T(8,128)(2,1)}, u32[]{:S(2)}, u32[]{:S(2)}) async-start(bf16[128,24,1024]{2,1,0:T(8,128)(2,1)} %bitcast.122), calls=%async_computation.2 | async-start | bytes 12582912 | tf_op jit(solution)/shard_map/all_to_all | solution.py:173
  180.8 6.0 %fusion.21 = bf16[704,1024]{1,0:T(8,128)(2,1)S(1)} fusion(bf16[1536,1024]{1,0:T(8,128)(2,1)} %bitcast.126, bf16[1,1536,704]{1,2,0:T(8,128)(2,1)} %param.19, bf16[1,1536,704]{1,2,0:T(8,128)(2,1)} %param.18), kind=kOutput, calls=%fused_computation.37 | convolution fusion | flops 2223964160 | bytes 8912896 | tf_op jit(solution)/shard_map/dot_general | solution.py:16
  186.9 2.8 %fusion.24 = bf16[704,1024]{1,0:T(8,128)(2,1)S(1)} fusion(bf16[1536,1024]{1,0:T(8,128)(2,1)S(1)} %bitcast.124, bf16[1,1536,704]{1,2,0:T(8,128)(2,1)S(1)} %copy-done.9, bf16[1,1536,704]{1,2,0:T(8,128)(2,1)S(1)} %copy-done.7), kind=kOutput, calls=%fused_computation.38 | convolution fusion | flops 2223964160 | bytes 8912896 | tf_op jit(solution)/shard_map/dot_general | solution.py:16
  189.6 1.8 maximum_bitcast_fusion.2
  191.5 4.6 %convolution_convert_fusion.1 = bf16[8,1024,192]{1,2,0:T(8,128)(2,1)S(1)} fusion(bf16[8,384,1024]{2,1,0:T(8,128)(2,1)} %bitcast.25, bf16[192,384]{1,0:T(8,128)(2,1)S(1)} %copy-done.1), kind=kOutput, calls=%fused_computation.30 | convolution fusion | flops 1209532416 | bytes 9584640 | tf_op jit(solution)/shard_map/dot_general | solution.py:181
  196.1 4.7 %convolution_convert_fusion = bf16[8,1024,192]{1,2,0:T(8,128)(2,1)S(1)} fusion(bf16[8,384,1024]{2,1,0:T(8,128)(2,1)} %bitcast.25, bf16[192,384]{1,0:T(8,128)(2,1)S(1)} %copy-done.2), kind=kOutput, calls=%fused_computation.29 | convolution fusion | flops 1209532416 | bytes 9584640 | tf_op jit(solution)/shard_map/dot_general | solution.py:181
  200.8 2.4 convolution_convert_fusion.7
  203.3 2.4 convolution_convert_fusion.5
  205.7 2.7 %convolution_convert_fusion.4 = bf16[1024,704]{0,1:T(8,128)(2,1)S(1)} fusion(bf16[1536,704]{0,1:T(8,128)(2,1)S(1)} %copy-done.13, bf16[1536,1024]{1,0:T(8,128)(2,1)S(1)} %bitcast.127), kind=kOutput, calls=%fused_computation.39 | convolution fusion | flops 2215313408 | bytes 6750208 | tf_op jit(solution)/shard_map/dot_general | solution.py:16
  208.4 2.4 convolution_convert_fusion.6
  210.8 2.8 %maximum_bitcast_fusion = (bf16[1,2048,704]{1,2,0:T(8,128)(2,1)}, bf16[1,2048,704]{1,2,0:T(8,128)(2,1)}) fusion(bf16[1024,704]{0,1:T(8,128)(2,1)S(1)} %convolution_convert_fusion.6, bf16[1024,704]{0,1:T(8,128)(2,1)S(1)} %convolution_convert_fusion.7, bf16[1024,704]{0,1:T(8,128)(2,1)S(1)} %convolution_convert_fusion.4, ...), kind=kLoop, calls=%fused_computation.26 | loop fusion | flops 11534336 | bytes 11534336 | tf_op jit(solution)/shard_map/broadcast_in_dim | solution.py:217
  213.7 42.4 %all-to-all-done.2 = bf16[128,24,1024]{2,1,0:T(8,128)(2,1)} async-done(((bf16[128,24,1024]{2,1,0:T(8,128)(2,1)}), bf16[128,24,1024]{2,1,0:T(8,128)(2,1)}, u32[]{:S(2)}, u32[]{:S(2)}) %all-to-all-start.2) | async-done | bytes 6291488 | tf_op jit(solution)/shard_map/all_to_all | solution.py:173
  256.1 5.5 %shard_map.140 = bf16[128,2048]{1,0:T(8,128)(2,1)} custom-call(s32[6,128]{1,0:T(8,128)} %bitcast.135, bf16[3072,1024]{1,0:T(8,128)(2,1)} %bitcast.24.refs_1_), custom_call_target="tpu_custom_call" | custom-call | flops 1610612736 | bytes 6291456 | tf_op jit(solution)/shard_map/pallas_call | solution.py:138
  (25 shorter events, 0.1 us)
Async XLA Ops:
  5.4 87.5 %all-to-all-start = ((bf16[128,24,1024]{2,1,0:T(8,128)(2,1)}), bf16[128,24,1024]{2,1,0:T(8,128)(2,1)}, u32[]{:S(2)}, u32[]{:S(2)}) async-start(bf16[128,24,1024]{2,1,0:T(8,128)(2,1)} %bitcast.121), calls=%async_computation | async-start | bytes 12582912 | tf_op jit(solution)/shard_map/all_to_all | solution.py:173
  92.9 6.5 %copy-start.1 = (bf16[192,384]{1,0:T(8,128)(2,1)S(1)}, bf16[192,384]{1,0:T(8,128)(2,1)}, u32[]{:S(2)}) copy-start(bf16[192,384]{1,0:T(8,128)(2,1)} %constant.6.clone) | copy-start | bytes 442372
  92.9 81.9 %all-to-all-start.1 = ((bf16[128,24,1024]{2,1,0:T(8,128)(2,1)}), bf16[128,24,1024]{2,1,0:T(8,128)(2,1)}, u32[]{:S(2)}, u32[]{:S(2)}) async-start(bf16[128,24,1024]{2,1,0:T(8,128)(2,1)} %bitcast.120), calls=%async_computation.1 | async-start | bytes 12582912 | tf_op jit(solution)/shard_map/all_to_all | solution.py:173
  99.4 4.6 %copy-start.2 = (bf16[192,384]{1,0:T(8,128)(2,1)S(1)}, bf16[192,384]{1,0:T(8,128)(2,1)}, u32[]{:S(2)}) copy-start(bf16[192,384]{1,0:T(8,128)(2,1)} %constant.7.clone) | copy-start | bytes 442372
  104.1 5.8 %copy-start = (bf16[8,1024,192]{1,2,0:T(8,128)(2,1)}, bf16[8,1024,192]{1,2,0:T(8,128)(2,1)S(1)}, u32[]{:S(2)}) copy-start(bf16[8,1024,192]{1,2,0:T(8,128)(2,1)S(1)} %convolution_convert_fusion.3) | copy-start | bytes 9437188
  104.1 5.8 %copy-start.3 = (bf16[1,704,2048]{2,1,0:T(8,128)(2,1)S(1)}, bf16[1,704,2048]{2,1,0:T(8,128)(2,1)}, u32[]{:S(2)}) copy-start(bf16[1,704,2048]{2,1,0:T(8,128)(2,1)} %param.17) | copy-start | bytes 8650756
  109.9 2.5 copy-start.6
  109.9 2.5 copy-start.8
  112.4 4.5 %copy-start.4 = (bf16[1,2048,704]{1,2,0:T(8,128)(2,1)S(1)}, bf16[1,2048,704]{1,2,0:T(8,128)(2,1)}, u32[]{:S(2)}) copy-start(bf16[1,2048,704]{1,2,0:T(8,128)(2,1)} %param.15) | copy-start | bytes 8650756
  116.8 2.7 %copy-start.10 = (bf16[1536,704]{0,1:T(8,128)(2,1)}, bf16[1536,704]{0,1:T(8,128)(2,1)S(1)}, u32[]{:S(2)}) copy-start(bf16[1536,704]{0,1:T(8,128)(2,1)S(1)} %get-tuple-element.13) | copy-start | bytes 6488068
  116.9 15.1 %copy-start.12 = (bf16[1536,704]{0,1:T(8,128)(2,1)}, bf16[1536,704]{0,1:T(8,128)(2,1)S(1)}, u32[]{:S(2)}) copy-start(bf16[1536,704]{0,1:T(8,128)(2,1)S(1)} %get-tuple-element.12) | copy-start | bytes 6488068
  119.6 2.7 %copy-start.5 = (bf16[1,2048,704]{1,2,0:T(8,128)(2,1)S(1)}, bf16[1,2048,704]{1,2,0:T(8,128)(2,1)}, u32[]{:S(2)}) copy-start(bf16[1,2048,704]{1,2,0:T(8,128)(2,1)} %param.16) | copy-start | bytes 8650756
  174.8 81.3 %all-to-all-start.2 = ((bf16[128,24,1024]{2,1,0:T(8,128)(2,1)}), bf16[128,24,1024]{2,1,0:T(8,128)(2,1)}, u32[]{:S(2)}, u32[]{:S(2)}) async-start(bf16[128,24,1024]{2,1,0:T(8,128)(2,1)} %bitcast.122), calls=%async_computation.2 | async-start | bytes 12582912 | tf_op jit(solution)/shard_map/all_to_all | solution.py:173
  180.8 6.1 %copy-start.7 = (bf16[1,1536,704]{1,2,0:T(8,128)(2,1)S(1)}, bf16[1,1536,704]{1,2,0:T(8,128)(2,1)}, u32[]{:S(2)}) copy-start(bf16[1,1536,704]{1,2,0:T(8,128)(2,1)} %param.18) | copy-start | bytes 6488068
  180.8 6.1 %copy-start.9 = (bf16[1,1536,704]{1,2,0:T(8,128)(2,1)S(1)}, bf16[1,1536,704]{1,2,0:T(8,128)(2,1)}, u32[]{:S(2)}) copy-start(bf16[1,1536,704]{1,2,0:T(8,128)(2,1)} %param.19) | copy-start | bytes 6488068
  196.1 4.8 %copy-start.11 = (bf16[1536,704]{0,1:T(8,128)(2,1)S(1)}, bf16[1536,704]{0,1:T(8,128)(2,1)}, u32[]{:S(2)}) copy-start(bf16[1536,704]{0,1:T(8,128)(2,1)} %copy-done.10) | copy-start | bytes 6488068
  200.8 2.4 copy-start.13
